TPU v7x, 128 devices: a whole 4x4x4 slice. The times are simulated.
128 devices in a mesh: dom: 128 (over z, y, x, core).
Axes of the slice: x: 4, y: 4, z: 4, core: 2. Of those that a mesh axis runs over, the one named last changes fastest.
Arguments:
- positions: float32 [3, 65536, 128], P(None, 'dom'), may hold values from 0 to 1
- velocities: float32 [3, 65536, 128], P(None, 'dom'), may hold values from -3 to 3
- masses: float32 [65536, 128], P('dom'), may hold values from 4.8828126e-05 to 0.00048828125
- active_leaves: int32 [2048], P('dom'), may hold values from 0 to 511, as said below
- active_count: int32 [128], P('dom'), may hold values from 4 to 16, as said below
- partner_owner: int32 [2048, 16], P('dom'), may hold values from 0 to 127, as said below
- partner_leaf: int32 [2048, 16], P('dom'), may hold values from 0 to 511, as said below
- mig_leaf: int32 [2048], P('dom'), may hold values from -1 to 511
Outputs:
- new_positions: float32 [3, 65536, 128], P(None, 'dom')
- new_velocities: float32 [3, 65536, 128], P(None, 'dom')
- arrived: float32 [7, 2048, 128], P(None, 'dom')
Inputs may be any that keep to these rules, and one draw needn't show every extreme that they name: `active_leaves`: within one domain's 16 slots the leaf numbers are distinct. `active_count`: at most 16; some domain has exactly 16. `partner_owner`: the owner lies within 2 domains of the list's own domain, counted cyclically along the curve. `partner_leaf`: for each domain and each other domain within reach, its lists name exactly 8 distinct leaves of that domain. `mig_leaf`: -1 marks an empty slot.
All inputs are finite; a program needn't handle non-finite values.
Results may differ from a plain program's by a relative error of at most 0.00002.
Values sent between devices are 32-bit elements; how exact they have to be, the bound alone decides.
No kernel may reach another device: no remote copies, remote signals or barrier semaphores. Data moves between devices by JAX's collectives and lax.ppermute only.
A program may use at most 64 MiB of HBM per device.

v0:
```python
import functools
import math

import jax
import jax.numpy as jnp
from jax import lax
from jax.experimental import pallas as pl
from jax.experimental.pallas import tpu as pltpu
from jax.sharding import PartitionSpec as P

REACH = 2
SLOTS = 4
IMPORT = 8
ACT = 16
PARTNERS = 16
LANES = 128
SIDES = 2 * REACH
IMPORTS = SIDES * IMPORT
BIG = 1 << 20
OWNER_BIT = 10
OWNER = 1 << OWNER_BIT

soften = 0.02
EPS = 4.0 * soften * soften
NEG_LOG2E = -math.log2(math.e)
TWO_OVER_ROOT_PI = 2.0 / math.sqrt(math.pi)

F32, BF16, I32 = jnp.float32, jnp.bfloat16, jnp.int32

CHUNK = 8
COARSE, ROWS = 16, 48
LISTS, LEAVES_OF, SIZES, FROM, LIVE, ACTIVE, MIG, PLAN = (0, 288), (576, 848), 1120, 1128, 1144, 1145, 1161, 1177
GIVEN = PLAN - LIVE
SLOT_BIT, PLACE_BIT = 16, 5
PLACES = 1023

VMEM = pl.BlockSpec(memory_space=pltpu.VMEM)
SMEM = pl.BlockSpec(memory_space=pltpu.SMEM)
ANY = pl.BlockSpec(memory_space=pl.ANY)


def params(mib):
    return pltpu.CompilerParams(vmem_limit_bytes=mib << 20)


def swapped(shard, partner):
    return lax.ppermute(shard, "dom", [(i, partner(i) % lax.axis_size("dom")) for i in range(lax.axis_size("dom"))])


PARTNERS_OF = (
    lambda d: d + 2 if d & 2 else d - 2,
    lambda d: d + 1 if d & 1 else d - 1,
    lambda d: d ^ 2,
    lambda d: d ^ 1,
)


def swap_offsets(me):
    one, two = 1 - 2 * (me & 1), 2 - 2 * (me & 2)
    return -two, -one, two, one


def number_of(offset):
    return offset + jnp.where(offset < 0, REACH, REACH - 1)


def request_kernel(domains, leaves, me_ref, entry_ref, *outs):
    requests, place_ref = outs[:SIDES], outs[SIDES]
    entry = entry_ref[...]
    leaf = entry & (OWNER - 1)
    relative = lax.shift_right_logical(entry, OWNER_BIT) - me_ref[0] + REACH
    relative = jnp.where(relative < 0, relative + domains, relative)
    relative = jnp.where(relative >= domains, relative - domains, relative)
    lane = lax.broadcasted_iota(I32, (1, LANES), 1)
    place = IMPORTS + leaf

    def over_all(reduce, v):
        return reduce(reduce(v, axis=0, keepdims=True), axis=1, keepdims=True)

    for side, offset in enumerate(swap_offsets(me_ref[0])):
        mine = relative == offset + REACH
        low, high = jnp.where(mine, leaf, BIG), jnp.where(mine, leaf, -1)
        rank = jnp.zeros_like(leaf)
        row = jnp.zeros((1, LANES), I32)
        for k in range(IMPORT // 2):
            last = IMPORT - 1 - k
            least, most = over_all(jnp.min, low), over_all(jnp.max, high)
            row = jnp.where(lane == k, jnp.broadcast_to(least, row.shape), row)
            row = jnp.where(lane == last, jnp.broadcast_to(most, row.shape), row)
            rank = jnp.where(low == least, k, jnp.where(high == most, last, rank))
            low = jnp.where(low == least, BIG, low)
            high = jnp.where(high == most, -1, high)
        requests[side][...] = jnp.clip(row, 0, leaves - 1)
        place = jnp.where(mine, side * IMPORT + rank, place)
    place_ref[...] = place


def plan_kernel(packed_ref, given_ref, _, plan_ref):
    for i in range(GIVEN):
        plan_ref[LIVE + i] = given_ref[i]
    live = given_ref[0]

    def one_slot(a, carried):
        ends, origins = carried
        leaf = given_ref[ACTIVE - LIVE + a]
        hits = jnp.int32(0)
        found = []
        for n in range(SIDES * SLOTS):
            hit = given_ref[MIG - LIVE + n] == leaf
            found.append(jnp.where(hit, a, origins[n]))
            hits = hits + jnp.where(hit, 1, 0)
        leaves = hits > 0
        end, local_end = (jnp.where(leaves, one, other) for one, other in zip(*ends))
        leaf_base = jnp.where(leaves, *LEAVES_OF)
        for k in range(PARTNERS):
            packed = packed_ref[a, k]
            place, times = lax.shift_right_logical(packed, PLACE_BIT), packed & 31
            remote = place < IMPORTS
            row = jnp.where(remote, place, IMPORTS + local_end - leaf_base)
            plan_ref[end] = (a << SLOT_BIT) + (row << PLACE_BIT) + times
            plan_ref[local_end] = place - IMPORTS
            counts = jnp.where(times > 0, 1, 0)
            end, local_end = end + counts, local_end + jnp.where(remote, 0, counts)
        one, other = ends
        leaving = tuple(jnp.where(leaves, new, old) for new, old in zip((end, local_end), one))
        staying = tuple(jnp.where(leaves, old, new) for new, old in zip((end, local_end), other))
        return (leaving, staying), tuple(found)

    starts = tuple((jnp.int32(base), jnp.int32(leaf_base)) for base, leaf_base in zip(LISTS, LEAVES_OF))
    nowhere = tuple(jnp.int32(-1) for _ in range(SIDES * SLOTS))
    ends, origins = lax.fori_loop(0, live, one_slot, (starts, nowhere))
    for n, a in enumerate(origins):
        plan_ref[FROM + n] = a
    for i, (end, local_end) in enumerate(ends):
        for k in range(2 * CHUNK):
            plan_ref[end + k] = 0
            plan_ref[local_end + k] = 0
        plan_ref[SIZES + 2 * i] = end - LISTS[i]
        plan_ref[SIZES + 2 * i + 1] = local_end - LEAVES_OF[i]


def reply_kernel(r0, r1, r2, r3, points, o0, o1, o2, o3, token):
    token[...] = jnp.zeros_like(token)
    for request, out in ((r0, o0), (r1, o1), (r2, o2), (r3, o3)):
        for k in range(IMPORT):
            at = pl.ds(request[0, k], 1)
            for c in range(3):
                out[8 * c + k : 8 * c + k + 1, :] = 2.0 * points[c, at, :]
            out[24 + k : 25 + k, :] = points[3, at, :]


def pieces(v):
    a = v.astype(BF16).astype(F32)
    b = (v - a).astype(BF16).astype(F32)
    return a, b, v - a - b


def split_rows(xs):
    h = [jnp.floor(x * 128.0 + 0.5) * (1.0 / 128.0) for x in xs]
    l = [x - y for x, y in zip(xs, h)]
    l1 = [v.astype(BF16).astype(F32) for v in l]
    l2 = [v - w for v, w in zip(l, l1)]
    coarse = h[0] * h[0] + h[1] * h[1] + h[2] * h[2]
    fine = sum(b * (2.0 * a + b) for a, b in zip(h, l))
    return h, l1, l2, coarse, fine


def times_minus_two(rows):
    return [-2.0 * r for r in rows]


def source_rows(xs):
    h, l1, l2, coarse, fine = split_rows(xs)
    one, none = jnp.ones_like(coarse), [None]
    first = times_minus_two(h) + [*pieces(coarse), one, one, one] + none * 7
    return first + [*h, *h, *l1, *l2, *l1, *l1, *l2, *l2, *pieces(fine), one, one, one] + none * 2


def target_rows(xs):
    h, l1, l2, coarse, fine = split_rows(xs)
    one, none = jnp.ones_like(coarse), [None]
    first = h + [one, one, one, *pieces(coarse)] + none * 7
    n1, n2, nh = times_minus_two(l1), times_minus_two(l2), times_minus_two(h)
    return first + [*n1, *n2, *nh, *nh, *n1, *n2, *n1, *n2, one, one, one, *pieces(fine + EPS)] + none * 2


def by_leaf(stage, rows, start=0):
    for r, row in enumerate(rows):
        stage[pl.ds(start + r, 8, stride=len(rows)), :] = jnp.zeros((8, LANES), F32) if row is None else row


def set_sources(first, xs, m, stage, sources, blocks):
    by_leaf(stage, source_rows(xs))
    pad = jnp.zeros((LANES - ROWS, LANES), F32)
    for k in range(8):
        wide = jnp.concatenate([stage[ROWS * k : ROWS * (k + 1), :], pad], axis=0)
        sources[first + k] = jnp.transpose(wide)[:, :ROWS].astype(BF16)
    rows = [*xs, jnp.ones_like(m), m] + [None] * 3
    by_leaf(blocks, rows, start=8 * first)


def run_list(plan_ref, base, n, targets, centers, sources, blocks, sums, square, split):
    def entry(q, t):
        at = q * CHUNK + t
        word = plan_ref[base + at]
        place = lax.shift_right_logical(word, PLACE_BIT) & PLACES
        return lax.shift_right_logical(word, SLOT_BIT), place, (word & 31).astype(F32)

    def distances(q):
        for t in range(CHUNK):
            slot, place, _ = entry(q, t)
            square[t] = jnp.dot(
                sources[place, :, :COARSE], targets[slot, :COARSE], preferred_element_type=F32
            ) + jnp.dot(sources[place, :, COARSE:], targets[slot, COARSE:], preferred_element_type=F32)

    def force_law():
        for t in range(CHUNK):
            sq = square[t]
            inverse = lax.rsqrt(sq)
            gauss = TWO_OVER_ROOT_PI * jnp.exp2(sq * NEG_LOG2E)
            law = ((1.0 - lax.erf(sq * inverse)) * inverse + gauss) * (inverse * inverse)
            high = law.astype(BF16)
            split[t, :LANES] = high
            split[t, LANES:] = (law - high.astype(F32)).astype(BF16)

    def add_up(q):
        for t in range(CHUNK):
            slot, place, times = entry(q, t)
            block = blocks[pl.ds(pl.multiple_of(8 * place, 8), 8), :]
            a, b, c = pieces((block - centers[slot]) * (block[4:5] * times))
            weights = jnp.concatenate([a, b, c, jnp.zeros_like(c)], axis=0).astype(BF16)
            out = jnp.dot(jnp.concatenate([weights, weights], axis=1), split[t], preferred_element_type=F32)
            sums[slot] += out[0:8] + out[8:16] + out[16:24]

    chunks = jnp.maximum(lax.shift_right_logical(n + CHUNK - 1, 3), 2)
    distances(0)
    force_law()
    distances(1)

    @pl.loop(2, chunks)
    def _(q):
        add_up(q - 2)
        force_law()
        distances(q)

    add_up(chunks - 2)
    force_law()
    add_up(chunks - 1)


def stage_kernel(given_ref, positions_ref, masses_ref, place_ref, points, targets, centers, packed_ref, held, stage):
    place = place_ref[...]
    column = lax.broadcasted_iota(I32, place.shape, 1)
    times = jnp.zeros_like(place)
    earlier = jnp.zeros_like(place)
    for k in range(PARTNERS):
        same = (place == place[:, k : k + 1]).astype(I32)
        times = times + same
        earlier = jnp.where(column > k, earlier + same, earlier)
    packed_ref[...] = (place << PLACE_BIT) + jnp.where(earlier > 0, 0, times)
    points[:3] = positions_ref[...]
    points[3] = masses_ref[...]
    for a in range(ACT):
        at = pl.ds(given_ref[ACTIVE - LIVE + a], 1)
        for c in range(3):
            held[16 * c + a : 16 * c + a + 1, :] = 2.0 * positions_ref[c, at, :]
    for g in range(ACT // 8):
        xs = [held[16 * c + 8 * g : 16 * c + 8 * g + 8, :] for c in range(3)]
        by_leaf(stage, target_rows(xs))
        for k in range(8):
            targets[8 * g + k] = stage[ROWS * k : ROWS * (k + 1), :].astype(BF16)
        means = [jnp.broadcast_to(jnp.mean(x, axis=1, keepdims=True), x.shape) for x in xs]
        by_leaf(stage, means + [None] * 5)
        for k in range(8):
            centers[8 * g + k] = stage[8 * k : 8 * k + 8, :]


def all_pairs(which, plan_ref, points, received, targets, centers, sums, held, stage, sources, blocks, square, split):
    for side, ref in enumerate(received):
        xs = [ref[8 * c : 8 * c + 8, :] for c in range(3)]
        set_sources(8 * side, xs, ref[24:32, :], stage, sources, blocks)

    @pl.loop(0, lax.shift_right_logical(plan_ref[SIZES + 2 * which + 1] + 7, 3))
    def _(g):
        for k in range(8):
            at = pl.ds(plan_ref[LEAVES_OF[which] + 8 * g + k], 1)
            for c in range(3):
                held[8 * c + k : 8 * c + k + 1, :] = 2.0 * points[c, at, :]
            held[24 + k : 25 + k, :] = points[3, at, :]
        xs = [held[8 * c : 8 * c + 8, :] for c in range(3)]
        first = pl.multiple_of(IMPORTS + 8 * g, 8)
        set_sources(first, xs, held[24:32, :], stage, sources, blocks)

    n = plan_ref[SIZES + 2 * which]
    run_list(plan_ref, LISTS[which], n, targets, centers, sources, blocks, sums, square, split)


def kicked(x, v, total, center, c):
    return v + (total[c : c + 1] - (2.0 * x - center[c : c + 1]) * total[3:4])


def leaving_kernel(me_ref, plan_ref, points, velocities_ref, targets, centers, r0, r1, r2, r3,
                   sums, b0, b1, b2, b3, *scratch):
    sums[...] = jnp.zeros_like(sums)

    @pl.when(plan_ref[SIZES] > 0)
    def _():
        all_pairs(0, plan_ref, points, (r0, r1, r2, r3), targets, centers, sums, *scratch)

    for offset, block in zip(swap_offsets(me_ref[0]), (b0, b1, b2, b3)):
        number = SLOTS * number_of(offset)
        for k in range(SLOTS):
            leaf, a = plan_ref[MIG + number + k], plan_ref[FROM + number + k]
            at = pl.ds(jnp.maximum(leaf, 0), 1)
            held = jnp.full((1, LANES), jnp.where(leaf >= 0, 1, 0), I32) > 0
            live = jnp.full((1, LANES), jnp.where(a >= 0, 1, 0), I32) > 0
            total, center = sums[jnp.maximum(a, 0)], centers[jnp.maximum(a, 0)]
            for c in range(3):
                x, v = points[c, at, :], velocities_ref[c, at, :]
                v = jnp.where(live, kicked(x, v, total, center, c), v)
                block[c, k : k + 1, :] = jnp.where(held, x + 0.25 * v, 0.0)
                block[3 + c, k : k + 1, :] = jnp.where(held, v, 0.0)
            block[6, k : k + 1, :] = jnp.where(held, points[3, at, :], 0.0)


def staying_kernel(plan_ref, points, velocities_ref, sums_in, targets, centers, r0, r1, r2, r3,
                   new_positions, new_velocities, sums, *scratch):
    sums[...] = sums_in[...]
    new_velocities[...] = velocities_ref[...]
    new_positions[...] = points[:3] + 0.25 * velocities_ref[...]
    all_pairs(1, plan_ref, points, (r0, r1, r2, r3), targets, centers, sums, *scratch)

    @pl.loop(0, plan_ref[LIVE])
    def _(a):
        at = pl.ds(plan_ref[ACTIVE + a], 1)
        total, center = sums[a], centers[a]
        for c in range(3):
            x = points[c, at, :]
            v = kicked(x, velocities_ref[c, at, :], total, center, c)
            new_velocities[c, at, :] = v
            new_positions[c, at, :] = x + 0.25 * v


def arrival_kernel(me_ref, c0, c1, c2, c3, out):
    for offset, came in zip(swap_offsets(me_ref[0]), (c0, c1, c2, c3)):
        out[:, pl.ds(SLOTS * number_of(-offset), SLOTS), :] = came[...]


def shape(*dims, dtype=F32):
    return jax.ShapeDtypeStruct(dims, dtype)


def per_device(positions, velocities, masses, active_leaves, active_count, partner_owner, partner_leaf, mig_leaf):
    leaves = positions.shape[1]
    domains = lax.axis_size("dom")
    me = lax.axis_index("dom").astype(I32)
    *requests, place = pl.pallas_call(
        functools.partial(request_kernel, domains, leaves),
        out_shape=[shape(1, LANES, dtype=I32)] * SIDES + [shape(ACT, PARTNERS, dtype=I32)],
        in_specs=[SMEM, VMEM],
        out_specs=[VMEM] * (SIDES + 1),
        compiler_params=params(4),
        cost_estimate=pl.CostEstimate(flops=3_000_000_000, bytes_accessed=10_000, transcendentals=0),
        name="requests",
    )(me.reshape(1), partner_owner * OWNER + partner_leaf)
    asked = [swapped(r, p) for r, p in zip(requests, PARTNERS_OF)]
    stage = [pltpu.VMEM((8 * ROWS, LANES), F32)]
    chunks = [pltpu.VMEM((CHUNK, LANES, LANES), F32), pltpu.VMEM((CHUNK, 2 * LANES, LANES), BF16)]
    slot_sums, most = shape(ACT, 8, LANES), IMPORTS + ACT * PARTNERS
    held = [pltpu.VMEM((48, LANES), F32)]
    given = jnp.concatenate([active_count, active_leaves, mig_leaf])
    points, targets, centers, packed = pl.pallas_call(
        stage_kernel,
        out_shape=[
            shape(4, leaves, LANES),
            shape(ACT, ROWS, LANES, dtype=BF16),
            slot_sums,
            shape(ACT, PARTNERS, dtype=I32),
        ],
        in_specs=[SMEM] + [VMEM] * 3,
        out_specs=[VMEM] * 4,
        scratch_shapes=held + stage,
        compiler_params=params(8),
        cost_estimate=pl.CostEstimate(flops=3_000_000_000, bytes_accessed=10_000, transcendentals=0),
        name="stage",
    )(given, positions, masses, place)
    *replies, token = pl.pallas_call(
        reply_kernel,
        out_shape=[shape(4 * IMPORT, LANES)] * SIDES + [shape(1, LANES)],
        in_specs=[SMEM] * SIDES + [VMEM],
        out_specs=[VMEM] * (SIDES + 1),
        compiler_params=params(4),
        name="replies",
    )(*asked, points)
    received = [swapped(r, p) for r, p in zip(replies, PARTNERS_OF)]
    plan = pl.pallas_call(
        plan_kernel,
        out_shape=shape(PLAN, dtype=I32),
        in_specs=[SMEM] * 2 + [ANY],
        out_specs=SMEM,
        compiler_params=params(4),
        cost_estimate=pl.CostEstimate(flops=2_000_000_000, bytes_accessed=10_000, transcendentals=0),
        name="plan",
    )(packed, given, token)
    tables = [pltpu.VMEM((most, LANES, ROWS), BF16), pltpu.VMEM((8 * most, LANES), F32)]
    sums, *blocks = pl.pallas_call(
        leaving_kernel,
        out_shape=[slot_sums] + [shape(7, SLOTS, LANES)] * SIDES,
        in_specs=[SMEM] * 2 + [VMEM] * (4 + SIDES),
        out_specs=[VMEM] * (1 + SIDES),
        scratch_shapes=held + stage + tables + chunks,
        compiler_params=params(24),
        name="leaving",
    )(me.reshape(1), plan, points, velocities, targets, centers, *received)
    came = [swapped(b, p) for b, p in zip(blocks, PARTNERS_OF)]
    new_positions, new_velocities = pl.pallas_call(
        staying_kernel,
        out_shape=[shape(3, leaves, LANES)] * 2,
        in_specs=[SMEM] + [VMEM] * (5 + SIDES),
        out_specs=[VMEM] * 2,
        scratch_shapes=[pltpu.VMEM((ACT, 8, LANES), F32)] + held + stage + tables + chunks,
        compiler_params=params(24),
        cost_estimate=pl.CostEstimate(flops=7_000_000_000, bytes_accessed=10_000, transcendentals=0),
        name="staying",
    )(plan, points, velocities, sums, targets, centers, *received)
    arrived = pl.pallas_call(
        arrival_kernel,
        out_shape=shape(7, SIDES * SLOTS, LANES),
        in_specs=[SMEM] + [VMEM] * SIDES,
        out_specs=VMEM,
        compiler_params=params(4),
        name="arrivals",
    )(me.reshape(1), *came)
    return new_positions, new_velocities, arrived


def solution(mesh):
    return jax.shard_map(
        per_device,
        mesh=mesh,
        in_specs=(
            P(None, "dom", None),
            P(None, "dom", None),
            P("dom", None),
            P("dom"),
            P("dom"),
            P("dom", None),
            P("dom", None),
            P("dom"),
        ),
        out_specs=(P(None, "dom", None), P(None, "dom", None), P(None, "dom", None)),
        check_vma=False,
    )
```

profile of v0, /device:TPU:1, one launch (start us, length us, event | category | flops | bytes accessed | tf_op | source)
XLA Modules:
  0.0 45.6 jit_solution(10932984673501309544)
XLA Ops:
  0.6 0.7 %multiply_add_fusion.entry_ref = s32[16,16]{1,0:T(8,128)S(1)} fusion(s32[16,16]{1,0:T(8,128)} %param.14, s32[16,16]{1,0:T(8,128)} %param.13), kind=kLoop, calls=%fused_computation | loop fusion | flops 512 | bytes 3072 | tf_op jit(solution)/shard_map/add | solution.py:365
  1.4 0.0 copy-start.1
  1.4 0.0 copy-start.2
  1.4 0.7 %requests.1 = (s32[1,128]{1,0:T(1,128)S(1)}, s32[1,128]{1,0:T(1,128)S(1)}, s32[1,128]{1,0:T(1,128)S(1)}, s32[1,128]{1,0:T(1,128)S(1)}, s32[16,16]{1,0:T(8,128)S(1)}) custom-call(s32[1]{0:T(128)} %bitcast.me_ref, s32[16,16]{1,0:T(8,128)S(1)} %multiply_add_fusion.entry_ref), custom_call_target="tpu_custom_call" | custom-call | flops 3000000000 | bytes 10000 | tf_op jit(solution)/shard_map/requests/pallas_call | solution.py:357
  2.1 9.3 %collective-permute-start = (s32[1,128]{1,0:T(1,128)S(1)}, s32[1,128]{1,0:T(1,128)S(1)}, u32[]{:S(2)}, u32[]{:S(2)}) collective-permute-start(s32[1,128]{1,0:T(1,128)S(1)} %get-tuple-element.26), channel_id=1, source_target_pairs={{0,126},{1,127},{2,4},{3,5},{4,2},{5,3},{6,8},{7,9},{8,6},{9,7},{1... | collective-permute-start | bytes 1544 | tf_op jit(solution)/shard_map/ppermute | solution.py:47
  11.4 0.0 collective-permute-start.1
  11.4 0.0 collective-permute-start.2
  11.4 0.0 copy-start.3
  11.4 0.0 copy-start.4
  11.4 2.1 %collective-permute-start.3 = (s32[1,128]{1,0:T(1,128)S(1)}, s32[1,128]{1,0:T(1,128)S(1)}, u32[]{:S(2)}, u32[]{:S(2)}) collective-permute-start(s32[1,128]{1,0:T(1,128)S(1)} %get-tuple-element.29), channel_id=1, source_target_pairs={{0,1},{1,0},{2,3},{3,2},{4,5},{5,4},{6,7},{7,6},{8,9},{9,8},{10,11... | collective-permute-start | bytes 1544 | tf_op jit(solution)/shard_map/ppermute | solution.py:47
  14.2 0.0 copy-done.3
  14.2 0.0 copy-done.4
  14.2 0.1 pad_add_fusion.given_ref
  14.3 0.0 copy-done.1
  14.3 0.0 copy-done.2
  14.3 0.8 %stage.1 = (f32[4,512,128]{2,1,0:T(8,128)S(1)}, bf16[16,48,128]{2,1,0:T(8,128)(2,1)S(1)}, f32[16,8,128]{2,1,0:T(8,128)S(1)}, s32[16,16]{1,0:T(8,128)S(1)}) custom-call(s32[33]{0:T(128)S(1)} %pad_add_fusion.given_ref, f32[3,512,128]{2,1,0:T(8,128)S(1)} %copy-done.1, f32[512,128]{1,0:T(8,128)S(1)} %copy-done.2, s32[16,16]{1,0:T(8,128)S(1)} %get-tuple-element.24.place_ref), custom_call_target="tpu_custom_call" | custom-call | flops 3000000000 | bytes 10000 | tf_op jit(solution)/shard_map/stage/pallas_call | solution.py:372
  15.1 0.0 collective-permute-done.r0
  15.1 0.0 collective-permute-done.1.r1
  15.1 0.0 collective-permute-done.2.r2
  15.1 0.0 collective-permute-done.3.r3
  15.1 0.6 %replies.1 = (f32[32,128]{1,0:T(8,128)S(1)}, f32[32,128]{1,0:T(8,128)S(1)}, f32[32,128]{1,0:T(8,128)S(1)}, f32[32,128]{1,0:T(8,128)S(1)}, f32[1,128]{1,0:T(1,128)S(1)}) custom-call(s32[1,128]{1,0:T(1,128)S(1)} %collective-permute-done.r0, s32[1,128]{1,0:T(1,128)S(1)} %collective-permute-done.1.r1, s32[1,128]{1,0:T(1,128)S(1)} %collective-permute-done.2.r2, ...), custom_call_target="tpu_custom_call" | custom-call | tf_op jit(solution)/shard_map/replies/pallas_call | solution.py:387
  15.8 6.4 %collective-permute-start.4 = (f32[32,128]{1,0:T(8,128)S(1)}, f32[32,128]{1,0:T(8,128)S(1)}, u32[]{:S(2)}, u32[]{:S(2)}) collective-permute-start(f32[32,128]{1,0:T(8,128)S(1)} %get-tuple-element.34), channel_id=1, source_target_pairs={{0,126},{1,127},{2,4},{3,5},{4,2},{5,3},{6,8},{7,9},{8,6},{9,7},{1... | collective-permute-start | bytes 49160 | tf_op jit(solution)/shard_map/ppermute | solution.py:47
  22.2 0.0 collective-permute-start.5
  22.2 0.0 collective-permute-start.6
  22.2 2.1 %collective-permute-start.7 = (f32[32,128]{1,0:T(8,128)S(1)}, f32[32,128]{1,0:T(8,128)S(1)}, u32[]{:S(2)}, u32[]{:S(2)}) collective-permute-start(f32[32,128]{1,0:T(8,128)S(1)} %get-tuple-element.37), channel_id=1, source_target_pairs={{0,1},{1,0},{2,3},{3,2},{4,5},{5,4},{6,7},{7,6},{8,9},{9,8},{10,11... | collective-permute-start | bytes 49160 | tf_op jit(solution)/shard_map/ppermute | solution.py:47
  24.4 0.0 copy-start
  24.4 2.5 %plan.1.plan_ref = s32[1177]{0:T(1024)S(1)} custom-call(s32[16,16]{1,0:T(8,128)S(1)} %get-tuple-element.25.packed_ref, s32[33]{0:T(128)S(1)} %pad_add_fusion.given_ref, f32[1,128]{1,0:T(1,128)S(1)} %get-tuple-element.31._), custom_call_target="tpu_custom_call" | custom-call | flops 2000000000 | bytes 10000 | tf_op jit(solution)/shard_map/plan/pallas_call | solution.py:396
  26.9 0.0 collective-permute-done.4.r0
  26.9 0.0 collective-permute-done.5.r1
  26.9 0.0 collective-permute-done.6.r2
  26.9 0.0 collective-permute-done.7.r3
  26.9 0.0 copy-done
  26.9 0.8 %leaving.1 = (f32[16,8,128]{2,1,0:T(8,128)S(1)}, f32[7,4,128]{2,1,0:T(4,128)S(1)}, f32[7,4,128]{2,1,0:T(4,128)S(1)}, f32[7,4,128]{2,1,0:T(4,128)S(1)}, f32[7,4,128]{2,1,0:T(4,128)S(1)}) custom-call(s32[1]{0:T(128)} %bitcast.me_ref, s32[1177]{0:T(1024)S(1)} %plan.1.plan_ref, f32[4,512,128]{2,1,0:T(8,128)S(1)} %get-tuple-element.30.points, ...), custom_call_target="tpu_custom_call" | custom-call | tf_op jit(solution)/shard_map/leaving/pallas_call | solution.py:406
  27.7 5.2 %collective-permute-start.8 = (f32[7,4,128]{2,1,0:T(4,128)S(1)}, f32[7,4,128]{2,1,0:T(4,128)S(1)}, u32[]{:S(2)}, u32[]{:S(2)}) collective-permute-start(f32[7,4,128]{2,1,0:T(4,128)S(1)} %get-tuple-element.41), channel_id=1, source_target_pairs={{0,126},{1,127},{2,4},{3,5},{4,2},{5,3},{6,8},{7,9},{8,6},{9,7},{1... | collective-permute-start | bytes 43016 | tf_op jit(solution)/shard_map/ppermute | solution.py:47
  32.9 0.0 collective-permute-start.9
  32.9 0.0 collective-permute-start.10
  32.9 3.0 %collective-permute-start.11 = (f32[7,4,128]{2,1,0:T(4,128)S(1)}, f32[7,4,128]{2,1,0:T(4,128)S(1)}, u32[]{:S(2)}, u32[]{:S(2)}) collective-permute-start(f32[7,4,128]{2,1,0:T(4,128)S(1)} %get-tuple-element.44), channel_id=1, source_target_pairs={{0,1},{1,0},{2,3},{3,2},{4,5},{5,4},{6,7},{7,6},{8,9},{9,8},{10,11... | collective-permute-start | bytes 43016 | tf_op jit(solution)/shard_map/ppermute | solution.py:47
  36.0 9.0 %staying.1 = (f32[3,512,128]{2,1,0:T(8,128)}, f32[3,512,128]{2,1,0:T(8,128)}) custom-call(s32[1177]{0:T(1024)S(1)} %plan.1.plan_ref, f32[4,512,128]{2,1,0:T(8,128)S(1)} %get-tuple-element.30.points, f32[3,512,128]{2,1,0:T(8,128)S(1)} %copy-done, f32[16,8,128]{2,1,0:T(8,128)S(1)} %get-tuple-element.38.sums_in, ...), custom_call_target="tpu_custom_call" | custom-call | flops 7000000000 | bytes 10000 | tf_op jit(solution)/shard_map/staying/pallas_call | solution.py:416
  44.9 0.0 collective-permute-done.8.c0
  44.9 0.0 collective-permute-done.9.c1
  44.9 0.0 collective-permute-done.10.c2
  44.9 0.0 collective-permute-done.11.c3
  45.0 0.6 %arrivals.1 = f32[7,16,128]{2,1,0:T(8,128)} custom-call(s32[1]{0:T(128)} %bitcast.me_ref, f32[7,4,128]{2,1,0:T(4,128)S(1)} %collective-permute-done.8.c0, f32[7,4,128]{2,1,0:T(4,128)S(1)} %collective-permute-done.9.c1, f32[7,4,128]{2,1,0:T(4,128)S(1)} %collective-permute-done.10.c2, f32[7,4,128]{2,1,0:T(4,128)S(1)} %collective-permute-done.11.c3), custom_call_target="tpu_custom_call" | custom-call | tf_op jit(solution)/shard_map/arrivals/pallas_call | solution.py:426
Async XLA Ops:
  1.4 12.9 %copy-start.1 = (f32[3,512,128]{2,1,0:T(8,128)S(1)}, f32[3,512,128]{2,1,0:T(8,128)}, u32[]{:S(2)}) copy-start(f32[3,512,128]{2,1,0:T(8,128)} %positions_ref.1) | copy-start | bytes 2359300
  1.4 12.9 %copy-start.2 = (f32[512,128]{1,0:T(8,128)S(1)}, f32[512,128]{1,0:T(8,128)}, u32[]{:S(2)}) copy-start(f32[512,128]{1,0:T(8,128)} %masses_ref.1) | copy-start | bytes 786436
  2.1 13.0 %collective-permute-start = (s32[1,128]{1,0:T(1,128)S(1)}, s32[1,128]{1,0:T(1,128)S(1)}, u32[]{:S(2)}, u32[]{:S(2)}) collective-permute-start(s32[1,128]{1,0:T(1,128)S(1)} %get-tuple-element.26), channel_id=1, source_target_pairs={{0,126},{1,127},{2,4},{3,5},{4,2},{5,3},{6,8},{7,9},{8,6},{9,7},{1... | collective-permute-start | bytes 1544 | tf_op jit(solution)/shard_map/ppermute | solution.py:47
  11.4 3.7 %collective-permute-start.1 = (s32[1,128]{1,0:T(1,128)S(1)}, s32[1,128]{1,0:T(1,128)S(1)}, u32[]{:S(2)}, u32[]{:S(2)}) collective-permute-start(s32[1,128]{1,0:T(1,128)S(1)} %get-tuple-element.27), channel_id=1, source_target_pairs={{0,127},{1,2},{2,1},{3,4},{4,3},{5,6},{6,5},{7,8},{8,7},{9,10},{10... | collective-permute-start | bytes 1544 | tf_op jit(solution)/shard_map/ppermute | solution.py:47
  11.4 3.7 %collective-permute-start.2 = (s32[1,128]{1,0:T(1,128)S(1)}, s32[1,128]{1,0:T(1,128)S(1)}, u32[]{:S(2)}, u32[]{:S(2)}) collective-permute-start(s32[1,128]{1,0:T(1,128)S(1)} %get-tuple-element.28), channel_id=1, source_target_pairs={{0,2},{1,3},{2,0},{3,1},{4,6},{5,7},{6,4},{7,5},{8,10},{9,11},{10,... | collective-permute-start | bytes 1544 | tf_op jit(solution)/shard_map/ppermute | solution.py:47
  11.4 2.8 %copy-start.3 = (s32[16]{0:T(128)S(1)}, s32[16]{0:T(128)}, u32[]{:S(2)}) copy-start(s32[16]{0:T(128)} %param.15) | copy-start | bytes 196
  11.4 2.8 %copy-start.4 = (s32[16]{0:T(128)S(1)}, s32[16]{0:T(128)}, u32[]{:S(2)}) copy-start(s32[16]{0:T(128)} %param.11) | copy-start | bytes 196
  11.4 3.7 %collective-permute-start.3 = (s32[1,128]{1,0:T(1,128)S(1)}, s32[1,128]{1,0:T(1,128)S(1)}, u32[]{:S(2)}, u32[]{:S(2)}) collective-permute-start(s32[1,128]{1,0:T(1,128)S(1)} %get-tuple-element.29), channel_id=1, source_target_pairs={{0,1},{1,0},{2,3},{3,2},{4,5},{5,4},{6,7},{7,6},{8,9},{9,8},{10,11... | collective-permute-start | bytes 1544 | tf_op jit(solution)/shard_map/ppermute | solution.py:47
  15.8 11.1 %collective-permute-start.4 = (f32[32,128]{1,0:T(8,128)S(1)}, f32[32,128]{1,0:T(8,128)S(1)}, u32[]{:S(2)}, u32[]{:S(2)}) collective-permute-start(f32[32,128]{1,0:T(8,128)S(1)} %get-tuple-element.34), channel_id=1, source_target_pairs={{0,126},{1,127},{2,4},{3,5},{4,2},{5,3},{6,8},{7,9},{8,6},{9,7},{1... | collective-permute-start | bytes 49160 | tf_op jit(solution)/shard_map/ppermute | solution.py:47
  22.2 4.7 %collective-permute-start.5 = (f32[32,128]{1,0:T(8,128)S(1)}, f32[32,128]{1,0:T(8,128)S(1)}, u32[]{:S(2)}, u32[]{:S(2)}) collective-permute-start(f32[32,128]{1,0:T(8,128)S(1)} %get-tuple-element.35), channel_id=1, source_target_pairs={{0,127},{1,2},{2,1},{3,4},{4,3},{5,6},{6,5},{7,8},{8,7},{9,10},{10... | collective-permute-start | bytes 49160 | tf_op jit(solution)/shard_map/ppermute | solution.py:47
  22.2 4.7 %collective-permute-start.6 = (f32[32,128]{1,0:T(8,128)S(1)}, f32[32,128]{1,0:T(8,128)S(1)}, u32[]{:S(2)}, u32[]{:S(2)}) collective-permute-start(f32[32,128]{1,0:T(8,128)S(1)} %get-tuple-element.36), channel_id=1, source_target_pairs={{0,2},{1,3},{2,0},{3,1},{4,6},{5,7},{6,4},{7,5},{8,10},{9,11},{10,... | collective-permute-start | bytes 49160 | tf_op jit(solution)/shard_map/ppermute | solution.py:47
  22.2 4.7 %collective-permute-start.7 = (f32[32,128]{1,0:T(8,128)S(1)}, f32[32,128]{1,0:T(8,128)S(1)}, u32[]{:S(2)}, u32[]{:S(2)}) collective-permute-start(f32[32,128]{1,0:T(8,128)S(1)} %get-tuple-element.37), channel_id=1, source_target_pairs={{0,1},{1,0},{2,3},{3,2},{4,5},{5,4},{6,7},{7,6},{8,9},{9,8},{10,11... | collective-permute-start | bytes 49160 | tf_op jit(solution)/shard_map/ppermute | solution.py:47
  24.4 2.5 %copy-start = (f32[3,512,128]{2,1,0:T(8,128)S(1)}, f32[3,512,128]{2,1,0:T(8,128)}, u32[]{:S(2)}) copy-start(f32[3,512,128]{2,1,0:T(8,128)} %velocities_ref.3) | copy-start | bytes 2359300
  27.7 17.2 %collective-permute-start.8 = (f32[7,4,128]{2,1,0:T(4,128)S(1)}, f32[7,4,128]{2,1,0:T(4,128)S(1)}, u32[]{:S(2)}, u32[]{:S(2)}) collective-permute-start(f32[7,4,128]{2,1,0:T(4,128)S(1)} %get-tuple-element.41), channel_id=1, source_target_pairs={{0,126},{1,127},{2,4},{3,5},{4,2},{5,3},{6,8},{7,9},{8,6},{9,7},{1... | collective-permute-start | bytes 43016 | tf_op jit(solution)/shard_map/ppermute | solution.py:47
  32.9 12.0 %collective-permute-start.9 = (f32[7,4,128]{2,1,0:T(4,128)S(1)}, f32[7,4,128]{2,1,0:T(4,128)S(1)}, u32[]{:S(2)}, u32[]{:S(2)}) collective-permute-start(f32[7,4,128]{2,1,0:T(4,128)S(1)} %get-tuple-element.42), channel_id=1, source_target_pairs={{0,127},{1,2},{2,1},{3,4},{4,3},{5,6},{6,5},{7,8},{8,7},{9,10},{10... | collective-permute-start | bytes 43016 | tf_op jit(solution)/shard_map/ppermute | solution.py:47
  32.9 12.0 %collective-permute-start.10 = (f32[7,4,128]{2,1,0:T(4,128)S(1)}, f32[7,4,128]{2,1,0:T(4,128)S(1)}, u32[]{:S(2)}, u32[]{:S(2)}) collective-permute-start(f32[7,4,128]{2,1,0:T(4,128)S(1)} %get-tuple-element.43), channel_id=1, source_target_pairs={{0,2},{1,3},{2,0},{3,1},{4,6},{5,7},{6,4},{7,5},{8,10},{9,11},{10,... | collective-permute-start | bytes 43016 | tf_op jit(solution)/shard_map/ppermute | solution.py:47
  32.9 12.0 %collective-permute-start.11 = (f32[7,4,128]{2,1,0:T(4,128)S(1)}, f32[7,4,128]{2,1,0:T(4,128)S(1)}, u32[]{:S(2)}, u32[]{:S(2)}) collective-permute-start(f32[7,4,128]{2,1,0:T(4,128)S(1)} %get-tuple-element.44), channel_id=1, source_target_pairs={{0,1},{1,0},{2,3},{3,2},{4,5},{5,4},{6,7},{7,6},{8,9},{9,8},{10,11... | collective-permute-start | bytes 43016 | tf_op jit(solution)/shard_map/ppermute | solution.py:47
where the time goes:
time: 45.8 us; the launch traced here: 45.6 us
  starting transfers between devices  28.3 us (62%)
  Pallas kernels  15 us (33%)
  between operations  1.44 us (3%)
  other arithmetic  0.8 us (2%)
    ppermute x12, starting transfers between devices, swapped(): lax.ppermute(shard, 'dom', [(i, partner(i) % lax.axis_size('dom')) for i...  28.3 us
    pallas_call x1, Pallas kernels, per_device(): pl.pallas_call(staying_kernel, out_shape=[shape(3, leaves, LANES)] * 2, i...  8.95 us
    pallas_call x1, Pallas kernels, per_device(): pl.pallas_call(plan_kernel, out_shape=shape(PLAN, dtype=I32), in_specs=[S...  2.5 us
  transfers between devices with their start and end apart: 12, of which 0 were waited for; matrix products, arithmetic and copies ran while one was open for 0% of the time, Pallas kernels for 27%

commit v1 on v0

--- a/solution.py
+++ b/solution.py
@@ -29,7 +29,8 @@
 
 CHUNK = 8
 COARSE, ROWS = 16, 48
-LISTS, LEAVES_OF, SIZES, FROM, LIVE, ACTIVE, MIG, PLAN = (0, 288), (576, 848), 1120, 1128, 1144, 1145, 1161, 1177
+LISTS, LEAVES_OF, SIZES, FROM, LIVE, ACTIVE, MIG, PLAN = (0, 288, 576), (864, 1136, 1408), 1680, 1688, 1704, 1705, 1721, 1737
+LEAVING, STAYING, EARLY = range(3)
 GIVEN = PLAN - LIVE
 SLOT_BIT, PLACE_BIT = 16, 5
 PLACES = 1023
@@ -95,9 +96,12 @@
     place_ref[...] = place
 
 
-def plan_kernel(packed_ref, given_ref, _, plan_ref):
-    for i in range(GIVEN):
-        plan_ref[LIVE + i] = given_ref[i]
+def early_place(me):
+    place = me & 7
+    return (place == 0) | ((place > 1) & (place < 6))
+
+
+def make_plan(early, packed_ref, given_ref, plan_ref):
     live = given_ref[0]
 
     def one_slot(a, carried):
@@ -110,21 +114,35 @@
             found.append(jnp.where(hit, a, origins[n]))
             hits = hits + jnp.where(hit, 1, 0)
         leaves = hits > 0
-        end, local_end = (jnp.where(leaves, one, other) for one, other in zip(*ends))
-        leaf_base = jnp.where(leaves, *LEAVES_OF)
+        slot = a << SLOT_BIT
+        one, other, local = ends
+        end, local_end = (jnp.where(leaves, *two) for two in zip(one, other))
+        leaf_base = jnp.where(leaves, *LEAVES_OF[:2])
+        own_end = local[0]
+        if early:
+            local_end, leaf_base = local[1], LEAVES_OF[EARLY]
         for k in range(PARTNERS):
             packed = packed_ref[a, k]
-            place, times = lax.shift_right_logical(packed, PLACE_BIT), packed & 31
-            remote = place < IMPORTS
-            row = jnp.where(remote, place, IMPORTS + local_end - leaf_base)
-            plan_ref[end] = (a << SLOT_BIT) + (row << PLACE_BIT) + times
-            plan_ref[local_end] = place - IMPORTS
-            counts = jnp.where(times > 0, 1, 0)
-            end, local_end = end + counts, local_end + jnp.where(remote, 0, counts)
-        one, other = ends
-        leaving = tuple(jnp.where(leaves, new, old) for new, old in zip((end, local_end), one))
-        staying = tuple(jnp.where(leaves, old, new) for new, old in zip((end, local_end), other))
-        return (leaving, staying), tuple(found)
+            counts = jnp.where((packed & 31) > 0, 1, 0)
+            remote = packed < (IMPORTS << PLACE_BIT)
+            own = jnp.where(remote, 0, counts)
+            at_home = slot + ((IMPORTS + local_end - leaf_base) << PLACE_BIT) + (packed & 31)
+            plan_ref[local_end] = lax.shift_right_logical(packed, PLACE_BIT) - IMPORTS
+            if early:
+                plan_ref[end] = slot + packed
+                plan_ref[own_end] = at_home
+                end, own_end = end + counts - own, own_end + own
+            else:
+                plan_ref[end] = jnp.where(remote, slot + packed, at_home)
+                end = end + counts
+            local_end = local_end + own
+        if early:
+            local, now = (own_end, local_end), (end, one[1])
+        else:
+            now = (end, local_end)
+        one = tuple(jnp.where(leaves, new, old) for new, old in zip(now, one))
+        other = tuple(jnp.where(leaves, old, new) for new, old in zip(now, other))
+        return (one, other, local), tuple(found)
 
     starts = tuple((jnp.int32(base), jnp.int32(leaf_base)) for base, leaf_base in zip(LISTS, LEAVES_OF))
     nowhere = tuple(jnp.int32(-1) for _ in range(SIDES * SLOTS))
@@ -132,11 +150,32 @@
     for n, a in enumerate(origins):
         plan_ref[FROM + n] = a
     for i, (end, local_end) in enumerate(ends):
+        if early and i != EARLY:
+            local_end = jnp.int32(LEAVES_OF[i])
         for k in range(2 * CHUNK):
-            plan_ref[end + k] = 0
+            plan_ref[end + k] = IMPORTS << PLACE_BIT if i == EARLY else 0
             plan_ref[local_end + k] = 0
         plan_ref[SIZES + 2 * i] = end - LISTS[i]
         plan_ref[SIZES + 2 * i + 1] = local_end - LEAVES_OF[i]
+
+
+def plan_kernel(me_ref, packed_ref, given_ref, points, targets, centers, _, plan_ref, sums, *scratch):
+    for i in range(GIVEN):
+        plan_ref[LIVE + i] = given_ref[i]
+    sums[...] = jnp.zeros_like(sums)
+    early = early_place(me_ref[0])
+
+    @pl.when(early)
+    def _():
+        make_plan(True, packed_ref, given_ref, plan_ref)
+
+        @pl.when(plan_ref[SIZES + 2 * EARLY] > 0)
+        def _():
+            all_pairs(EARLY, plan_ref, points, (), targets, centers, sums, *scratch)
+
+    @pl.when(jnp.logical_not(early))
+    def _():
+        make_plan(False, packed_ref, given_ref, plan_ref)
 
 
 def reply_kernel(r0, r1, r2, r3, points, o0, o1, o2, o3, token):
@@ -191,10 +230,8 @@
 
 def set_sources(first, xs, m, stage, sources, blocks):
     by_leaf(stage, source_rows(xs))
-    pad = jnp.zeros((LANES - ROWS, LANES), F32)
     for k in range(8):
-        wide = jnp.concatenate([stage[ROWS * k : ROWS * (k + 1), :], pad], axis=0)
-        sources[first + k] = jnp.transpose(wide)[:, :ROWS].astype(BF16)
+        sources[first + k] = jnp.transpose(stage[ROWS * k : ROWS * (k + 1), :]).astype(BF16)
     rows = [*xs, jnp.ones_like(m), m] + [None] * 3
     by_leaf(blocks, rows, start=8 * first)
 
@@ -299,13 +336,13 @@
     return v + (total[c : c + 1] - (2.0 * x - center[c : c + 1]) * total[3:4])
 
 
-def leaving_kernel(me_ref, plan_ref, points, velocities_ref, targets, centers, r0, r1, r2, r3,
+def leaving_kernel(me_ref, plan_ref, points, velocities_ref, sums_in, targets, centers, r0, r1, r2, r3,
                    sums, b0, b1, b2, b3, *scratch):
-    sums[...] = jnp.zeros_like(sums)
+    sums[...] = sums_in[...]
 
     @pl.when(plan_ref[SIZES] > 0)
     def _():
-        all_pairs(0, plan_ref, points, (r0, r1, r2, r3), targets, centers, sums, *scratch)
+        all_pairs(LEAVING, plan_ref, points, (r0, r1, r2, r3), targets, centers, sums, *scratch)
 
     for offset, block in zip(swap_offsets(me_ref[0]), (b0, b1, b2, b3)):
         number = SLOTS * number_of(offset)
@@ -328,7 +365,7 @@
     sums[...] = sums_in[...]
     new_velocities[...] = velocities_ref[...]
     new_positions[...] = points[:3] + 0.25 * velocities_ref[...]
-    all_pairs(1, plan_ref, points, (r0, r1, r2, r3), targets, centers, sums, *scratch)
+    all_pairs(STAYING, plan_ref, points, (r0, r1, r2, r3), targets, centers, sums, *scratch)
 
     @pl.loop(0, plan_ref[LIVE])
     def _(a):
@@ -393,25 +430,26 @@
         name="replies",
     )(*asked, points)
     received = [swapped(r, p) for r, p in zip(replies, PARTNERS_OF)]
-    plan = pl.pallas_call(
+    tables = [pltpu.VMEM((most, LANES, ROWS), BF16), pltpu.VMEM((8 * most, LANES), F32)]
+    plan, sums = pl.pallas_call(
         plan_kernel,
-        out_shape=shape(PLAN, dtype=I32),
-        in_specs=[SMEM] * 2 + [ANY],
-        out_specs=SMEM,
-        compiler_params=params(4),
-        cost_estimate=pl.CostEstimate(flops=2_000_000_000, bytes_accessed=10_000, transcendentals=0),
+        out_shape=[shape(PLAN, dtype=I32), slot_sums],
+        in_specs=[SMEM] * 3 + [VMEM] * 3 + [ANY],
+        out_specs=[SMEM, VMEM],
+        scratch_shapes=held + stage + tables + chunks,
+        compiler_params=params(24),
+        cost_estimate=pl.CostEstimate(flops=4_000_000_000, bytes_accessed=10_000, transcendentals=0),
         name="plan",
-    )(packed, given, token)
-    tables = [pltpu.VMEM((most, LANES, ROWS), BF16), pltpu.VMEM((8 * most, LANES), F32)]
+    )(me.reshape(1), packed, given, points, targets, centers, token)
     sums, *blocks = pl.pallas_call(
         leaving_kernel,
         out_shape=[slot_sums] + [shape(7, SLOTS, LANES)] * SIDES,
-        in_specs=[SMEM] * 2 + [VMEM] * (4 + SIDES),
+        in_specs=[SMEM] * 2 + [VMEM] * (5 + SIDES),
         out_specs=[VMEM] * (1 + SIDES),
         scratch_shapes=held + stage + tables + chunks,
         compiler_params=params(24),
         name="leaving",
-    )(me.reshape(1), plan, points, velocities, targets, centers, *received)
+    )(me.reshape(1), plan, points, velocities, sums, targets, centers, *received)
     came = [swapped(b, p) for b, p in zip(blocks, PARTNERS_OF)]
     new_positions, new_velocities = pl.pallas_call(
         staying_kernel,

time: 45.8 us -> 46.3 us (1.011); the launches traced: 45.6 us -> 45.6 us
  starting transfers between devices: 28.3 us -> 27.7 us
  Pallas kernels: 15 us -> 15.6 us
    ppermute x12, starting transfers between devices: 28.3 us -> 27.7 us  [swapped(): lax.ppermute(shard, 'dom', [(i, partner(i) % lax.axis_size('dom')) for i...]
  transfers between devices with their start and end apart: 12 -> 12, of which waited for: 0 -> 0; matrix products, arithmetic and copies ran while one was open for 0% -> 0% of each run, Pallas kernels for 27% -> 28%
where the time goes in v1:
time: 46.3 us; the launch traced here: 45.6 us
  starting transfers between devices  27.7 us (60%)
  Pallas kernels  15.6 us (34%)
  between operations  1.44 us (3%)
  other arithmetic  0.8 us (2%)
    ppermute x12, starting transfers between devices, swapped(): lax.ppermute(shard, 'dom', [(i, partner(i) % lax.axis_size('dom')) for i...  27.7 us
    pallas_call x1, Pallas kernels, per_device(): pl.pallas_call(staying_kernel, out_shape=[shape(3, leaves, LANES)] * 2, i...  9.26 us
    pallas_call x1, Pallas kernels, per_device(): pl.pallas_call(plan_kernel, out_shape=[shape(PLAN, dtype=I32), slot_sums]...  2.74 us
  transfers between devices with their start and end apart: 12, of which 0 were waited for; matrix products, arithmetic and copies ran while one was open for 0% of the time, Pallas kernels for 28%

profile of v1, /device:TPU:1, one launch (start us, length us, event | category | flops | bytes accessed | tf_op | source)
XLA Modules:
  0.0 45.6 jit_solution(6522427502926073014)
XLA Ops:
  0.6 0.7 %multiply_add_fusion.entry_ref = s32[16,16]{1,0:T(8,128)S(1)} fusion(s32[16,16]{1,0:T(8,128)} %param.14, s32[16,16]{1,0:T(8,128)} %param.13), kind=kLoop, calls=%fused_computation | loop fusion | flops 512 | bytes 3072 | tf_op jit(solution)/shard_map/add | solution.py:402
  1.4 0.0 copy-start.1
  1.4 0.0 copy-start.2
  1.4 0.7 %requests.1 = (s32[1,128]{1,0:T(1,128)S(1)}, s32[1,128]{1,0:T(1,128)S(1)}, s32[1,128]{1,0:T(1,128)S(1)}, s32[1,128]{1,0:T(1,128)S(1)}, s32[16,16]{1,0:T(8,128)S(1)}) custom-call(s32[1]{0:T(128)} %bitcast.me_ref, s32[16,16]{1,0:T(8,128)S(1)} %multiply_add_fusion.entry_ref), custom_call_target="tpu_custom_call" | custom-call | flops 3000000000 | bytes 10000 | tf_op jit(solution)/shard_map/requests/pallas_call | solution.py:394
  2.1 9.3 %collective-permute-start = (s32[1,128]{1,0:T(1,128)S(1)}, s32[1,128]{1,0:T(1,128)S(1)}, u32[]{:S(2)}, u32[]{:S(2)}) collective-permute-start(s32[1,128]{1,0:T(1,128)S(1)} %get-tuple-element.31), channel_id=1, source_target_pairs={{0,126},{1,127},{2,4},{3,5},{4,2},{5,3},{6,8},{7,9},{8,6},{9,7},{1... | collective-permute-start | bytes 1544 | tf_op jit(solution)/shard_map/ppermute | solution.py:48
  11.4 0.0 collective-permute-start.1
  11.4 0.0 collective-permute-start.2
  11.4 0.0 copy-start.3
  11.4 0.0 copy-start.4
  11.4 2.1 %collective-permute-start.3 = (s32[1,128]{1,0:T(1,128)S(1)}, s32[1,128]{1,0:T(1,128)S(1)}, u32[]{:S(2)}, u32[]{:S(2)}) collective-permute-start(s32[1,128]{1,0:T(1,128)S(1)} %get-tuple-element.34), channel_id=1, source_target_pairs={{0,1},{1,0},{2,3},{3,2},{4,5},{5,4},{6,7},{7,6},{8,9},{9,8},{10,11... | collective-permute-start | bytes 1544 | tf_op jit(solution)/shard_map/ppermute | solution.py:48
  14.2 0.0 copy-done.3
  14.2 0.0 copy-done.4
  14.2 0.1 pad_add_fusion.given_ref
  14.3 0.0 copy-done.1
  14.3 0.0 copy-done.2
  14.3 0.8 %stage.1 = (f32[4,512,128]{2,1,0:T(8,128)S(1)}, bf16[16,48,128]{2,1,0:T(8,128)(2,1)S(1)}, f32[16,8,128]{2,1,0:T(8,128)S(1)}, s32[16,16]{1,0:T(8,128)S(1)}) custom-call(s32[33]{0:T(128)S(1)} %pad_add_fusion.given_ref, f32[3,512,128]{2,1,0:T(8,128)S(1)} %copy-done.1, f32[512,128]{1,0:T(8,128)S(1)} %copy-done.2, s32[16,16]{1,0:T(8,128)S(1)} %get-tuple-element.26.place_ref), custom_call_target="tpu_custom_call" | custom-call | flops 3000000000 | bytes 10000 | tf_op jit(solution)/shard_map/stage/pallas_call | solution.py:409
  15.1 0.0 collective-permute-done.r0
  15.1 0.0 collective-permute-done.1.r1
  15.1 0.0 collective-permute-done.2.r2
  15.1 0.0 collective-permute-done.3.r3
  15.1 0.6 %replies.1 = (f32[32,128]{1,0:T(8,128)S(1)}, f32[32,128]{1,0:T(8,128)S(1)}, f32[32,128]{1,0:T(8,128)S(1)}, f32[32,128]{1,0:T(8,128)S(1)}, f32[1,128]{1,0:T(1,128)S(1)}) custom-call(s32[1,128]{1,0:T(1,128)S(1)} %collective-permute-done.r0, s32[1,128]{1,0:T(1,128)S(1)} %collective-permute-done.1.r1, s32[1,128]{1,0:T(1,128)S(1)} %collective-permute-done.2.r2, ...), custom_call_target="tpu_custom_call" | custom-call | tf_op jit(solution)/shard_map/replies/pallas_call | solution.py:424
  15.8 6.4 %collective-permute-start.4 = (f32[32,128]{1,0:T(8,128)S(1)}, f32[32,128]{1,0:T(8,128)S(1)}, u32[]{:S(2)}, u32[]{:S(2)}) collective-permute-start(f32[32,128]{1,0:T(8,128)S(1)} %get-tuple-element.38), channel_id=1, source_target_pairs={{0,126},{1,127},{2,4},{3,5},{4,2},{5,3},{6,8},{7,9},{8,6},{9,7},{1... | collective-permute-start | bytes 49160 | tf_op jit(solution)/shard_map/ppermute | solution.py:48
  22.2 0.0 collective-permute-start.5
  22.2 0.0 collective-permute-start.6
  22.2 2.1 %collective-permute-start.7 = (f32[32,128]{1,0:T(8,128)S(1)}, f32[32,128]{1,0:T(8,128)S(1)}, u32[]{:S(2)}, u32[]{:S(2)}) collective-permute-start(f32[32,128]{1,0:T(8,128)S(1)} %get-tuple-element.41), channel_id=1, source_target_pairs={{0,1},{1,0},{2,3},{3,2},{4,5},{5,4},{6,7},{7,6},{8,9},{9,8},{10,11... | collective-permute-start | bytes 49160 | tf_op jit(solution)/shard_map/ppermute | solution.py:48
  24.4 0.0 copy-start
  24.4 2.7 %plan.1 = (s32[1737]{0:T(1024)S(1)}, f32[16,8,128]{2,1,0:T(8,128)S(1)}) custom-call(s32[1]{0:T(128)} %bitcast.me_ref, s32[16,16]{1,0:T(8,128)S(1)} %get-tuple-element.27.packed_ref, s32[33]{0:T(128)S(1)} %pad_add_fusion.given_ref, f32[4,512,128]{2,1,0:T(8,128)S(1)} %get-tuple-element.28.points, bf16[16,48,128]{2,1,0:T(8,128)(2,1)S(1)} %get-tuple-element.29.targets, ...), custom_call_target="tpu_custom_call" | custom-call | flops 4000000000 | bytes 10000 | tf_op jit(solution)/shard_map/plan/pallas_call | solution.py:434
  27.1 0.0 collective-permute-done.4.r0
  27.1 0.0 collective-permute-done.5.r1
  27.1 0.0 collective-permute-done.6.r2
  27.1 0.0 collective-permute-done.7.r3
  27.2 0.0 copy-done
  27.2 0.8 %leaving.1 = (f32[16,8,128]{2,1,0:T(8,128)S(1)}, f32[7,4,128]{2,1,0:T(4,128)S(1)}, f32[7,4,128]{2,1,0:T(4,128)S(1)}, f32[7,4,128]{2,1,0:T(4,128)S(1)}, f32[7,4,128]{2,1,0:T(4,128)S(1)}) custom-call(s32[1]{0:T(128)} %bitcast.me_ref, s32[1737]{0:T(1024)S(1)} %get-tuple-element.36.plan_ref, f32[4,512,128]{2,1,0:T(8,128)S(1)} %get-tuple-element.28.points, ...), custom_call_target="tpu_custom_call" | custom-call | tf_op jit(solution)/shard_map/leaving/pallas_call | solution.py:444
  28.0 5.5 %collective-permute-start.8 = (f32[7,4,128]{2,1,0:T(4,128)S(1)}, f32[7,4,128]{2,1,0:T(4,128)S(1)}, u32[]{:S(2)}, u32[]{:S(2)}) collective-permute-start(f32[7,4,128]{2,1,0:T(4,128)S(1)} %get-tuple-element.45), channel_id=1, source_target_pairs={{0,126},{1,127},{2,4},{3,5},{4,2},{5,3},{6,8},{7,9},{8,6},{9,7},{1... | collective-permute-start | bytes 43016 | tf_op jit(solution)/shard_map/ppermute | solution.py:48
  33.5 0.0 collective-permute-start.9
  33.5 0.0 collective-permute-start.10
  33.5 2.1 %collective-permute-start.11 = (f32[7,4,128]{2,1,0:T(4,128)S(1)}, f32[7,4,128]{2,1,0:T(4,128)S(1)}, u32[]{:S(2)}, u32[]{:S(2)}) collective-permute-start(f32[7,4,128]{2,1,0:T(4,128)S(1)} %get-tuple-element.48), channel_id=1, source_target_pairs={{0,1},{1,0},{2,3},{3,2},{4,5},{5,4},{6,7},{7,6},{8,9},{9,8},{10,11... | collective-permute-start | bytes 43016 | tf_op jit(solution)/shard_map/ppermute | solution.py:48
  35.7 9.3 %staying.1 = (f32[3,512,128]{2,1,0:T(8,128)}, f32[3,512,128]{2,1,0:T(8,128)}) custom-call(s32[1737]{0:T(1024)S(1)} %get-tuple-element.36.plan_ref, f32[4,512,128]{2,1,0:T(8,128)S(1)} %get-tuple-element.28.points, f32[3,512,128]{2,1,0:T(8,128)S(1)} %copy-done, f32[16,8,128]{2,1,0:T(8,128)S(1)} %get-tuple-element.42.sums_in, ...), custom_call_target="tpu_custom_call" | custom-call | flops 7000000000 | bytes 10000 | tf_op jit(solution)/shard_map/staying/pallas_call | solution.py:454
  44.9 0.0 collective-permute-done.8.c0
  44.9 0.0 collective-permute-done.9.c1
  44.9 0.0 collective-permute-done.10.c2
  44.9 0.0 collective-permute-done.11.c3
  44.9 0.6 %arrivals.1 = f32[7,16,128]{2,1,0:T(8,128)} custom-call(s32[1]{0:T(128)} %bitcast.me_ref, f32[7,4,128]{2,1,0:T(4,128)S(1)} %collective-permute-done.8.c0, f32[7,4,128]{2,1,0:T(4,128)S(1)} %collective-permute-done.9.c1, f32[7,4,128]{2,1,0:T(4,128)S(1)} %collective-permute-done.10.c2, f32[7,4,128]{2,1,0:T(4,128)S(1)} %collective-permute-done.11.c3), custom_call_target="tpu_custom_call" | custom-call | tf_op jit(solution)/shard_map/arrivals/pallas_call | solution.py:464
Async XLA Ops:
  1.4 12.9 %copy-start.1 = (f32[3,512,128]{2,1,0:T(8,128)S(1)}, f32[3,512,128]{2,1,0:T(8,128)}, u32[]{:S(2)}) copy-start(f32[3,512,128]{2,1,0:T(8,128)} %positions_ref.1) | copy-start | bytes 2359300
  1.4 12.9 %copy-start.2 = (f32[512,128]{1,0:T(8,128)S(1)}, f32[512,128]{1,0:T(8,128)}, u32[]{:S(2)}) copy-start(f32[512,128]{1,0:T(8,128)} %masses_ref.1) | copy-start | bytes 786436
  2.1 13.0 %collective-permute-start = (s32[1,128]{1,0:T(1,128)S(1)}, s32[1,128]{1,0:T(1,128)S(1)}, u32[]{:S(2)}, u32[]{:S(2)}) collective-permute-start(s32[1,128]{1,0:T(1,128)S(1)} %get-tuple-element.31), channel_id=1, source_target_pairs={{0,126},{1,127},{2,4},{3,5},{4,2},{5,3},{6,8},{7,9},{8,6},{9,7},{1... | collective-permute-start | bytes 1544 | tf_op jit(solution)/shard_map/ppermute | solution.py:48
  11.4 3.7 %collective-permute-start.1 = (s32[1,128]{1,0:T(1,128)S(1)}, s32[1,128]{1,0:T(1,128)S(1)}, u32[]{:S(2)}, u32[]{:S(2)}) collective-permute-start(s32[1,128]{1,0:T(1,128)S(1)} %get-tuple-element.32), channel_id=1, source_target_pairs={{0,127},{1,2},{2,1},{3,4},{4,3},{5,6},{6,5},{7,8},{8,7},{9,10},{10... | collective-permute-start | bytes 1544 | tf_op jit(solution)/shard_map/ppermute | solution.py:48
  11.4 3.7 %collective-permute-start.2 = (s32[1,128]{1,0:T(1,128)S(1)}, s32[1,128]{1,0:T(1,128)S(1)}, u32[]{:S(2)}, u32[]{:S(2)}) collective-permute-start(s32[1,128]{1,0:T(1,128)S(1)} %get-tuple-element.33), channel_id=1, source_target_pairs={{0,2},{1,3},{2,0},{3,1},{4,6},{5,7},{6,4},{7,5},{8,10},{9,11},{10,... | collective-permute-start | bytes 1544 | tf_op jit(solution)/shard_map/ppermute | solution.py:48
  11.4 2.8 %copy-start.3 = (s32[16]{0:T(128)S(1)}, s32[16]{0:T(128)}, u32[]{:S(2)}) copy-start(s32[16]{0:T(128)} %param.15) | copy-start | bytes 196
  11.4 2.8 %copy-start.4 = (s32[16]{0:T(128)S(1)}, s32[16]{0:T(128)}, u32[]{:S(2)}) copy-start(s32[16]{0:T(128)} %param.11) | copy-start | bytes 196
  11.4 3.7 %collective-permute-start.3 = (s32[1,128]{1,0:T(1,128)S(1)}, s32[1,128]{1,0:T(1,128)S(1)}, u32[]{:S(2)}, u32[]{:S(2)}) collective-permute-start(s32[1,128]{1,0:T(1,128)S(1)} %get-tuple-element.34), channel_id=1, source_target_pairs={{0,1},{1,0},{2,3},{3,2},{4,5},{5,4},{6,7},{7,6},{8,9},{9,8},{10,11... | collective-permute-start | bytes 1544 | tf_op jit(solution)/shard_map/ppermute | solution.py:48
  15.8 11.3 %collective-permute-start.4 = (f32[32,128]{1,0:T(8,128)S(1)}, f32[32,128]{1,0:T(8,128)S(1)}, u32[]{:S(2)}, u32[]{:S(2)}) collective-permute-start(f32[32,128]{1,0:T(8,128)S(1)} %get-tuple-element.38), channel_id=1, source_target_pairs={{0,126},{1,127},{2,4},{3,5},{4,2},{5,3},{6,8},{7,9},{8,6},{9,7},{1... | collective-permute-start | bytes 49160 | tf_op jit(solution)/shard_map/ppermute | solution.py:48
  22.2 4.9 %collective-permute-start.5 = (f32[32,128]{1,0:T(8,128)S(1)}, f32[32,128]{1,0:T(8,128)S(1)}, u32[]{:S(2)}, u32[]{:S(2)}) collective-permute-start(f32[32,128]{1,0:T(8,128)S(1)} %get-tuple-element.39), channel_id=1, source_target_pairs={{0,127},{1,2},{2,1},{3,4},{4,3},{5,6},{6,5},{7,8},{8,7},{9,10},{10... | collective-permute-start | bytes 49160 | tf_op jit(solution)/shard_map/ppermute | solution.py:48
  22.2 4.9 %collective-permute-start.6 = (f32[32,128]{1,0:T(8,128)S(1)}, f32[32,128]{1,0:T(8,128)S(1)}, u32[]{:S(2)}, u32[]{:S(2)}) collective-permute-start(f32[32,128]{1,0:T(8,128)S(1)} %get-tuple-element.40), channel_id=1, source_target_pairs={{0,2},{1,3},{2,0},{3,1},{4,6},{5,7},{6,4},{7,5},{8,10},{9,11},{10,... | collective-permute-start | bytes 49160 | tf_op jit(solution)/shard_map/ppermute | solution.py:48
  22.2 4.9 %collective-permute-start.7 = (f32[32,128]{1,0:T(8,128)S(1)}, f32[32,128]{1,0:T(8,128)S(1)}, u32[]{:S(2)}, u32[]{:S(2)}) collective-permute-start(f32[32,128]{1,0:T(8,128)S(1)} %get-tuple-element.41), channel_id=1, source_target_pairs={{0,1},{1,0},{2,3},{3,2},{4,5},{5,4},{6,7},{7,6},{8,9},{9,8},{10,11... | collective-permute-start | bytes 49160 | tf_op jit(solution)/shard_map/ppermute | solution.py:48
  24.4 2.8 %copy-start = (f32[3,512,128]{2,1,0:T(8,128)S(1)}, f32[3,512,128]{2,1,0:T(8,128)}, u32[]{:S(2)}) copy-start(f32[3,512,128]{2,1,0:T(8,128)} %velocities_ref.3) | copy-start | bytes 2359300
  28.0 16.9 %collective-permute-start.8 = (f32[7,4,128]{2,1,0:T(4,128)S(1)}, f32[7,4,128]{2,1,0:T(4,128)S(1)}, u32[]{:S(2)}, u32[]{:S(2)}) collective-permute-start(f32[7,4,128]{2,1,0:T(4,128)S(1)} %get-tuple-element.45), channel_id=1, source_target_pairs={{0,126},{1,127},{2,4},{3,5},{4,2},{5,3},{6,8},{7,9},{8,6},{9,7},{1... | collective-permute-start | bytes 43016 | tf_op jit(solution)/shard_map/ppermute | solution.py:48
  33.5 11.4 %collective-permute-start.9 = (f32[7,4,128]{2,1,0:T(4,128)S(1)}, f32[7,4,128]{2,1,0:T(4,128)S(1)}, u32[]{:S(2)}, u32[]{:S(2)}) collective-permute-start(f32[7,4,128]{2,1,0:T(4,128)S(1)} %get-tuple-element.46), channel_id=1, source_target_pairs={{0,127},{1,2},{2,1},{3,4},{4,3},{5,6},{6,5},{7,8},{8,7},{9,10},{10... | collective-permute-start | bytes 43016 | tf_op jit(solution)/shard_map/ppermute | solution.py:48
  33.5 11.4 %collective-permute-start.10 = (f32[7,4,128]{2,1,0:T(4,128)S(1)}, f32[7,4,128]{2,1,0:T(4,128)S(1)}, u32[]{:S(2)}, u32[]{:S(2)}) collective-permute-start(f32[7,4,128]{2,1,0:T(4,128)S(1)} %get-tuple-element.47), channel_id=1, source_target_pairs={{0,2},{1,3},{2,0},{3,1},{4,6},{5,7},{6,4},{7,5},{8,10},{9,11},{10,... | collective-permute-start | bytes 43016 | tf_op jit(solution)/shard_map/ppermute | solution.py:48
  33.5 11.4 %collective-permute-start.11 = (f32[7,4,128]{2,1,0:T(4,128)S(1)}, f32[7,4,128]{2,1,0:T(4,128)S(1)}, u32[]{:S(2)}, u32[]{:S(2)}) collective-permute-start(f32[7,4,128]{2,1,0:T(4,128)S(1)} %get-tuple-element.48), channel_id=1, source_target_pairs={{0,1},{1,0},{2,3},{3,2},{4,5},{5,4},{6,7},{7,6},{8,9},{9,8},{10,11... | collective-permute-start | bytes 43016 | tf_op jit(solution)/shard_map/ppermute | solution.py:48
